TPU v7x, 1024 devices: a whole 4x8x16 slice. The times are simulated.
1024 devices in a mesh: head: 8 (over x, z_hi), seq: 128 (over z_lo, y, core).
Axes of the slice: x: 4, y: 8, z: 16 (z_hi: 2, z_lo: 8; z = z_hi * 8 + z_lo), core: 2. Of those that a mesh axis runs over, the one named last changes fastest.
Arguments:
- queries: bfloat16 [128, 128, 576], P('seq', 'head'), may hold values from -400 to 400
- query_pos: int32 [128], replicated, may hold values from 32259 to 32767, as said below
- latents: bfloat16 [32768, 576], P('seq'), may hold values from -6 to 6
- valid_keys: int32 [128], P('seq'), may hold values from 128 to 256, as said below
- output_gradient: bfloat16 [128, 128, 512], P('seq', 'head'), may hold values from -600 to 600
- kv_down: bfloat16 [7168, 576], P('head'), may hold values from -0.0625 to 0.0625
Outputs:
- latent_grad: float32 [32768, 576], P('seq')
- input_grad: bfloat16 [32768, 7168], P('seq', 'head')
Inputs may be any that keep to these rules, and one draw needn't show every extreme that they name: `query_pos`: positions rise strictly with the query index, consecutive ones differ by 1 to 4, and the last is 32767. The first valid_keys[s] positions of shard s are valid; some shard is full and some holds exactly half.
All inputs are finite; a program needn't handle non-finite values.
Results may differ from a plain program's by a relative error of at most 0.015.
Values may be sent and summed in bfloat16 or wider, within the bound.
A program may use at most 32 MiB of HBM per device.

v0:
```python
import jax
import jax.numpy as jnp
from jax import lax
from jax.sharding import Mesh
from jax.sharding import PartitionSpec as P

SEQ = ("seq_0", "seq_1", "seq_2")


score_scale = 192.0 ** (-0.5)


def sent_together(arrays, axis, dim, along):
    widths = [a.shape[along] for a in arrays]
    both = jnp.concatenate(arrays, axis=along)
    whole = lax.all_gather(both, axis, axis=dim, tiled=True)
    return tuple(jnp.split(whole, [sum(widths[:k]) for k in range(1, len(widths))], axis=along))


def gathered_once(value, axis):
    leaves = jax.tree.leaves(value)
    sequence = sorted(range(len(leaves)), key=lambda k: -leaves[k].size)
    width = (1, *leaves[sequence[0]].shape)[-1]
    lines = [
        jnp.pad(leaves[k].reshape(-1), (0, -leaves[k].size % width)).reshape(-1, width)
        for k in sequence
    ]
    both, at, found = (lax.all_gather(jnp.concatenate(lines), axis), 0, {})
    for k, line in zip(sequence, lines):
        share = both[:, at : at + len(line)].reshape(len(both), -1)
        found[k] = share[:, : leaves[k].size].reshape(-1, *leaves[k].shape)
        at += len(line)
    numbers = iter(range(len(leaves)))
    return jax.tree.map(lambda _: found[next(numbers)], value)


def merged_by_axis(value, axes, combine):
    for axis in axes:
        pieces = gathered_once(value, axis)
        value = jax.tree.map(lambda part: part[0], pieces)
        for k in range(1, lax.axis_size(axis)):
            value = combine(value, jax.tree.map(lambda part: part[k], pieces))
    return value


def in_blocks(value, dim, devices):
    before, after = (value.shape[:dim], value.shape[dim + 1 :])
    return jnp.moveaxis(value.reshape(*before, devices, -1, *after), dim, 0)


def sum_at_owner(value, axis, dim):
    devices = lax.axis_size(axis)
    parts = lax.all_to_all(in_blocks(value, dim, devices), axis, 0, 0, tiled=True)
    return jnp.sum(parts.astype(jnp.float32), axis=0)


def in_order(parts, dim):
    parts = jnp.moveaxis(parts, 0, dim)
    dims = parts.shape
    return parts.reshape(*dims[:dim], dims[dim] * dims[dim + 1], *dims[dim + 2 :])


def sent_to_all(value, axis):
    devices = lax.axis_size(axis)
    return lax.all_to_all(
        jnp.broadcast_to(value[None], (devices, *value.shape)), axis, 0, 0, tiled=True
    )


def gather_directly(value, axis, dim):
    return in_order(sent_to_all(value, axis), dim)


def join_triple(first_part, second_part):
    top = jnp.maximum(first_part[0], second_part[0])
    first_weight = jnp.exp(first_part[0] - top)
    second_weight = jnp.exp(second_part[0] - top)
    return (
        top,
        first_part[1] * first_weight + second_part[1] * second_weight,
        first_part[2] * first_weight + second_part[2] * second_weight,
    )


def shards(queries, query_pos, latents, valid_keys, output_gradient, kv_down):
    key_count = latents.shape[0]
    latent_span = output_gradient.shape[2]
    all_query, gradient_total = sent_together((queries, output_gradient), SEQ, 0, 2)
    first_key = lax.axis_index(SEQ) * key_count
    local_index = jnp.arange(key_count, dtype=jnp.int32)
    key_pos = first_key + local_index
    visible = (local_index < valid_keys[0])[None, :] & (key_pos[None, :] <= query_pos[:, None])
    visible = visible[:, None, :]
    scores = (
        jnp.einsum("qhc,kc->qhk", all_query, latents, preferred_element_type=jnp.float32)
        * score_scale
    )
    scores = jnp.where(visible, scores, -1e30)
    local_max = jnp.max(scores, axis=-1)
    shifted = jnp.where(visible, jnp.exp(scores - local_max[..., None]), 0.0)
    local_total = jnp.sum(shifted, axis=-1)
    dprobs = jnp.einsum(
        "mcg,dg->mcd", gradient_total, latents[:, :latent_span], preferred_element_type=jnp.float32
    )
    local_weighted = jnp.sum(shifted * dprobs, axis=-1)
    row_max, row_total, row_weighted = merged_by_axis(
        (local_max, local_total, local_weighted), SEQ, join_triple
    )
    lse = row_max + jnp.log(row_total)
    probs = jnp.where(visible, jnp.exp(scores - lse[..., None]), 0.0)
    delta_rows = row_weighted / row_total
    dscores = probs * (dprobs - delta_rows[..., None])
    probs_b = probs.astype(jnp.bfloat16)
    dscores_b = dscores.astype(jnp.bfloat16)
    key_contribution = (
        jnp.einsum("qhk,qhc->kc", dscores_b, all_query, preferred_element_type=jnp.float32)
        * score_scale
    )
    value_contribution = jnp.einsum(
        "qhk,qhv->kv", probs_b, gradient_total, preferred_element_type=jnp.float32
    )
    owned = sum_at_owner(
        jnp.concatenate(
            [
                key_contribution[:, :latent_span] + value_contribution,
                key_contribution[:, latent_span:],
            ],
            axis=1,
        ).astype(jnp.bfloat16),
        "head",
        0,
    )
    latent_grad = gather_directly(owned.astype(jnp.bfloat16), "head", 0).astype(owned.dtype)
    input_grad = lax.dot_general(
        latent_grad.astype(jnp.bfloat16),
        kv_down,
        (((1,), (1,)), ((), ())),
        preferred_element_type=jnp.float32,
    ).astype(jnp.bfloat16)
    return (latent_grad, input_grad)


def solution(mesh):
    torus = Mesh(
        mesh.devices.reshape(mesh.shape["head"], 8, 8, 2), ("head", "seq_0", "seq_1", "seq_2")
    )
    placed = (
        P(SEQ, "head", None),
        P(),
        P(SEQ, None),
        P(SEQ),
        P(SEQ, "head", None),
        P("head", None),
    )
    return jax.shard_map(
        shards,
        mesh=torus,
        in_specs=placed,
        out_specs=(P(SEQ, None), P(SEQ, "head")),
        check_vma=False,
    )
```

profile of v0, /device:TPU:8, one launch (start us, length us, event | category | flops | bytes accessed | tf_op | source)
XLA Modules:
  0.0 410.8 jit_solution(6757026638531000670)
XLA Ops:
  7.2 0.0 copy-start
  7.2 0.0 all-gather.5.cloned.1.call-start
  7.2 1.5 pad_maximum_fusion.1
  8.7 0.0 all-gather.5.cloned.1.call-update
  9.4 0.7 compare_and_fusion
  10.2 238.6 %all-gather.5.cloned.1.call-done = bf16[128,16,1088]{2,1,0:T(8,128)(2,1)} async-done(((bf16[1,16,1088]{2,1,0:T(8,128)(2,1)}), bf16[128,16,1088]{2,1,0:T(8,128)(2,1)}) %all-gather.5.cloned.1.call-update) | async-done | bytes 4456464 | tf_op jit(solution)/shard_map/all_gather | solution.py:16
  248.8 3.5 split.8
  252.3 3.9 copy.260
  256.3 2.1 fusion.34
  258.4 0.0 copy-start.1
  258.4 0.0 copy-start.5
  258.4 3.6 split.9
  262.0 0.0 copy-start.3
  262.0 0.0 copy-done.1
  262.0 0.0 copy-done.5
  262.0 4.4 %fusion.4 = (f32[128,16]{0,1:T(8,128)S(1)}, f32[128,16]{0,1:T(8,128)S(1)}, f32[128,16,256]{2,0,1:T(8,128)}) fusion(f32[128,16,256]{2,0,1:T(8,128)S(1)} %get-tuple-element.85, f32[128,16]{0,1:T(8,128)S(1)} %get-tuple-element.84, pred[128,256]{1,0:T(8,128)(4,1)S(1)} %compare_and_fusion, bf16[256,576]{0,1:T(8,128)(2,1)S(1)} %copy-done.5, ...), kind=kOutput, calls=%fused_computation.9 | convolution fusion | flops 539488256 | bytes 6610944 | tf_op jit(solution)/shard_map/mcg,dg->mcd/dot_general | solution.py:102
  266.4 0.0 copy-done.3
  266.4 46.6 %all-gather = f32[3072,16]{0,1:T(8,128)S(1)} all-gather(f32[384,16]{0,1:T(8,128)S(1)} %pad_maximum_fusion.2), channel_id=2, replica_groups=mesh['head'=8,'seq_0'=8,'seq_1'=8,'seq_2'=2] {'seq_0'}, dimensions={0}, use_global_device_ids=true | all-gather | bytes 221184 | tf_op jit(solution)/shard_map/all_gather | solution.py:28
  313.1 0.1 fusion.31
  313.4 23.5 %all-gather.1 = f32[3072,16]{0,1:T(8,128)S(1)} all-gather(f32[384,16]{0,1:T(8,128)S(1)} %pad_maximum_fusion.3), channel_id=3, replica_groups=mesh['head'=8,'seq_0'=8,'seq_1'=8,'seq_2'=2] {'seq_1'}, dimensions={0}, use_global_device_ids=true | all-gather | bytes 221184 | tf_op jit(solution)/shard_map/all_gather | solution.py:28
  337.0 0.1 fusion.29
  337.2 1.8 all-gather.2
  339.1 0.0 copy-start.2
  339.1 0.0 copy-start.4
  339.1 3.3 fusion.6
  342.5 0.0 copy-done.2
  342.5 0.1 copy-done.4
  342.6 2.8 fusion.13
  345.4 0.1 copy.254
  345.6 0.1 copy.255
  345.7 29.0 %all_to_all.10 = bf16[8,32,576]{2,1,0:T(8,128)(2,1)S(1)} all-to-all(bf16[8,32,576]{2,1,0:T(8,128)(2,1)S(1)} %pad_maximum_fusion), channel_id=1, replica_groups=mesh['head'=8,'seq_0'=8,'seq_1'=8,'seq_2'=2] {'head'}, dimensions={0} | all-to-all | bytes 589824 | tf_op jit(solution)/shard_map/all_to_all | solution.py:53
  374.7 0.1 reduce_sum.32
  374.8 26.7 %all_to_all.11 = bf16[8,32,576]{2,1,0:T(8,128)(2,1)S(1)} all-to-all(bf16[8,32,576]{2,1,0:T(8,128)(2,1)S(1)} %broadcast_in_dim.38), channel_id=1, replica_groups=mesh['head'=8,'seq_0'=8,'seq_1'=8,'seq_2'=2] {'head'}, dimensions={0} | all-to-all | bytes 589824 | tf_op jit(solution)/shard_map/all_to_all | solution.py:65
  401.5 0.1 bitcast_convert_fusion
  401.6 1.0 copy.256
  402.6 0.0 copy-done
  402.6 1.3 convolution_convert_fusion
  (19 shorter events, 0.5 us)
Async XLA Ops:
  7.2 395.5 %copy-start = (bf16[896,576]{0,1:T(8,128)(2,1)S(1)}, bf16[896,576]{0,1:T(8,128)(2,1)}, u32[]{:S(2)}) copy-start(bf16[896,576]{0,1:T(8,128)(2,1)} %param.11) | copy-start | bytes 3096580
  7.2 241.7 %all-gather.5.cloned.1.call-start = ((), (), s32[]{:S(2)}) async-start(), calls=%async_computation.2 | async-start | bytes 4755456 | tf_op jit(solution)/shard_map/all_gather | solution.py:16
  258.4 3.6 copy-start.1
  258.4 3.6 copy-start.5
  262.0 4.5 %copy-start.3 = (bf16[128,16,512]{2,1,0:T(8,128)(2,1)}, bf16[128,16,512]{2,1,0:T(8,128)(2,1)S(1)}, u32[]{:S(2)}) copy-start(bf16[128,16,512]{2,1,0:T(8,128)(2,1)S(1)} %split.9) | copy-start | bytes 6291460
  339.1 3.4 copy-start.2
  339.1 3.5 copy-start.4
Sparse Core Ops, SparseCore 0:
  11.3 237.4 all-gather.4
where the time goes:
time: 411 us
  waiting for transfers between devices  239 us (58%)
  blocking collectives  128 us (31%)
  between operations  14.9 us (4%)
  matrix products  14 us (3%)
  local copies, waits for them, and re-layouts  12.9 us (3%)
    all_gather x1, waiting for transfers between devices, sent_together(): whole = lax.all_gather(both, axis, axis=dim, tiled=True)  239 us
    all_gather x3, blocking collectives, gathered_once(): both, at, found = (lax.all_gather(jnp.concatenate(lines), axis), 0, {})  72 us
    all_to_all x1, blocking collectives, sum_at_owner(): lax.all_to_all(in_blocks(value, dim, devices), axis, 0, 0, tiled=True)  29 us
    all_to_all x1, blocking collectives, sent_to_all(): lax.all_to_all(jnp.broadcast_to(value[None], (devices, *value.shape)), ax...  26.7 us
  transfers between devices with their start and end apart: 1, of which 1 were waited for; matrix products, arithmetic and copies ran while one was open for 0% of the time, Pallas kernels for 0%

commit v1 on v0

v1 whole, which is shorter than its diff:
```python
import jax
import jax.numpy as jnp
from jax import lax
from jax.experimental import pallas as pl
from jax.experimental.pallas import tpu as pltpu
from jax.sharding import Mesh
from jax.sharding import PartitionSpec as P

AXES = ("x", "zh", "zl", "y", "c")
HEAD = ("x", "zh")
SEQ = ("zl", "y", "c")
NX, NZ, NY = 4, 8, 8
HEADS = 16
KEYS = 256
VAL = 512
LAT = 576
BLOCK = 1152
SPAN = NY * HEADS
PART = 288
SPLIT = ((0, 128), (128, 160))
MESH = pl.DeviceIdType.MESH

score_scale = 192.0 ** (-0.5)


def at(**moved):
    return tuple(moved[a] if a in moved else lax.axis_index(a) for a in AXES)


def dot(a, b):
    return jnp.dot(a, b, preferred_element_type=jnp.float32)


def dot_t(a, b):
    return lax.dot_general(a, b, (((1,), (1,)), ((), ())), preferred_element_type=jnp.float32)


def kernel(
    qpos_ref, valid_ref, q_ref, g_ref, lat_ref, out_ref,
    rows, keys, krot, vis, pbuf, dbuf, pb, dsb, stat, stat_z, stat_y, stat_f,
    s1, r1, s2, r2, s3, r3, fin,
    g_recv, g_send, k_recv, k_send, z_recv, z_send, y_recv, y_send, f_recv, f_send,
    r1_recv, r1_send, r2_recv, r2_send, r3_recv, r3_send, r4_recv, r4_send,
):
    x, zh, zl, y, c = (lax.axis_index(a) for a in AXES)
    mine = zl * NY + y
    y_up, y_down = lax.rem(y + 1, NY), lax.rem(y + NY - 1, NY)

    def remote(src, dst, send, recv, to):
        return pltpu.make_async_remote_copy(
            src_ref=src, dst_ref=dst, send_sem=send, recv_sem=recv, device_id=to, device_id_type=MESH
        )

    y_peers = [at(y=lax.rem(y + d, NY)) for d in range(1, NY)]
    z_peers = [lax.rem(zl + d, NZ) for d in range(1, NZ)]
    x_peers = [lax.rem(x + d, NX) for d in range(1, NX)]
    sibling = at(c=1 - c)
    across = at(zh=1 - zh)

    barrier = pltpu.get_barrier_semaphore()
    everyone = (
        y_peers + [at(zl=z) for z in z_peers] + [at(x=k) for k in x_peers] + [sibling, across]
    )
    for peer in everyone:
        pl.semaphore_signal(barrier, inc=1, device_id=peer, device_id_type=MESH)

    rows[mine, :, 0:VAL] = q_ref[0, :, 0:VAL]
    rows[mine, :, VAL : 2 * VAL] = g_ref[0]
    rot = q_ref[0, :, VAL:LAT]
    rows[mine, :, 2 * VAL : BLOCK] = jnp.concatenate([rot, rot], axis=1)
    keys[c, :, 0:VAL] = lat_ref[:, 0:VAL]
    local = lax.broadcasted_iota(jnp.int32, (KEYS, 64), 0)
    flag = jnp.where(local < valid_ref[0], 1.0, 0.0).astype(jnp.bfloat16)
    keys[c, :, VAL:640] = jnp.concatenate([lat_ref[:, VAL:LAT], flag], axis=1)

    pl.semaphore_wait(barrier, len(everyone))

    def send_rows(source, to):
        remote(rows.at[source], rows.at[source], g_send.at[0], g_recv.at[source], to).start()

    def wait_rows(source):
        remote(rows.at[source], rows.at[source], g_send.at[0], g_recv.at[source], sibling).wait_recv()

    send_rows(mine, at(y=y_up))
    send_rows(mine, at(y=y_down))
    for d in range(1, NZ):
        pl.when(zl + d < NZ)(lambda: send_rows(mine, at(zl=zl + d)))
        pl.when(zl - d >= 0)(lambda: send_rows(mine, at(zl=zl - d)))
    swap = remote(keys.at[c], keys.at[c], k_send.at[0], k_recv.at[0], sibling)
    swap.start()
    swap.wait_recv()
    for half in range(2):
        tail = keys[half, :, VAL:640].astype(jnp.float32)
        lane = lax.broadcasted_iota(jnp.int32, (KEYS, 128), 1)
        krot[half * KEYS : (half + 1) * KEYS] = jnp.where(lane < 64, tail, 0.0).astype(jnp.bfloat16)
        vis[half * KEYS : (half + 1) * KEYS] = jnp.broadcast_to(tail[:, 64:65], (KEYS, 128))

    def first_pass(zs):
        chunk = rows.at[pl.ds(zs * NY, NY)]
        values = keys[:, :, 0:VAL].reshape(2 * KEYS, VAL)
        s = dot_t(values, chunk[:, :, 0:VAL].reshape(SPAN, VAL))
        s = s + dot_t(krot[...], chunk[:, :, 2 * VAL : BLOCK].reshape(SPAN, 128))
        lane = lax.broadcasted_iota(jnp.int32, (1, SPAN), 1)
        qpos = jnp.zeros((1, SPAN), jnp.int32)
        for k in range(NY):
            qpos = jnp.where(lane // HEADS == k, qpos_ref[zs * 2 * NY + 2 * k + c], qpos)
        key_pos = lax.broadcasted_iota(jnp.int32, (2 * KEYS, SPAN), 0) + mine * 2 * KEYS
        seen = (vis[...] > 0.5) & (key_pos <= qpos)
        s = jnp.where(seen, s * score_scale, -1e30)
        top = jnp.maximum(jnp.max(s, axis=0, keepdims=True), -1e20)
        p = jnp.exp(s - top)
        dp = dot_t(values, chunk[:, :, VAL : 2 * VAL].reshape(SPAN, VAL))
        pbuf[zs] = p
        dbuf[zs] = dp
        stat[zs, 0:1] = top
        stat[zs, 1:2] = jnp.sum(p, axis=0, keepdims=True)
        stat[zs, 2:3] = jnp.sum(p * dp, axis=0, keepdims=True)
        stat[zs, 3:8] = jnp.zeros((5, SPAN), jnp.float32)

        @pl.when(zs != zl)
        def _():
            remote(
                stat.at[zs], stat_z.at[zl], z_send.at[0], z_recv.at[zl], at(zl=zs)
            ).start()

    def slots(group, work):
        def body(k, _):
            d = 2 * group + k // 2
            zs = jnp.where(k % 2 == 0, zl + d, zl - d)
            ok = (d >= 0) & (zs >= 0) & (zs < NZ) & ((d < NZ) & ((d > 0) | (k % 2 == 0)))
            pl.when(ok)(lambda: work(zs))
            return 0

        lax.fori_loop(0, 4, body, 0)

    def inject(zs):
        @pl.when(zs != zl)
        def _():
            source = zs * NY + y
            wait_rows(source)
            send_rows(source, at(y=y_up))
            send_rows(source, at(y=y_down))

    def pass_on(e):
        def work(zs):
            even = lax.rem(zs, 2) == 0
            rising = zs * NY + lax.rem(y + NY - e, NY)
            falling = zs * NY + lax.rem(y + e, NY)
            if e <= 3:
                wait_rows(rising)
                if e < 3:
                    send_rows(rising, at(y=y_up))
                else:
                    pl.when(even)(lambda: send_rows(rising, at(y=y_up)))
                wait_rows(falling)
                if e < 3:
                    send_rows(falling, at(y=y_down))
                else:
                    pl.when(jnp.logical_not(even))(lambda: send_rows(falling, at(y=y_down)))
            else:
                wait_rows(rising)

        return work

    def step(t, _):
        slots(t, inject)
        for e in range(1, 5):
            pl.when((t - e >= 0) & (t - e <= 3))(lambda e=e: slots(t - e, pass_on(e)))
        pl.when(t >= 4)(lambda: slots(t - 4, first_pass))
        return 0

    lax.fori_loop(0, 8, step, 0)

    def merged(parts):
        top = parts[0][0:1]
        for part in parts[1:]:
            top = jnp.maximum(top, part[0:1])
        total = jnp.zeros_like(top)
        weighted = jnp.zeros_like(top)
        for part in parts:
            gain = jnp.exp(part[0:1] - top)
            total = total + part[1:2] * gain
            weighted = weighted + part[2:3] * gain
        return top, total, weighted

    stat_z[zl] = stat[zl]
    for z in z_peers:
        remote(stat.at[0], stat_z.at[z], z_send.at[0], z_recv.at[z], sibling).wait_recv()
    top, total, weighted = merged([stat_z[k] for k in range(NZ)])
    stat_y[y, 0:1] = top
    stat_y[y, 1:2] = total
    stat_y[y, 2:3] = weighted
    stat_y[y, 3:8] = jnp.zeros((5, SPAN), jnp.float32)
    for d in range(1, NY):
        remote(
            stat_y.at[y], stat_y.at[y], y_send.at[0], y_recv.at[y], at(y=lax.rem(y + d, NY))
        ).start()
    for d in range(1, NY):
        k = lax.rem(y + d, NY)
        remote(stat_y.at[k], stat_y.at[k], y_send.at[0], y_recv.at[k], sibling).wait_recv()
    top, total, weighted = merged([stat_y[k] for k in range(NY)])
    stat_f[zl, 0:1] = top + jnp.log(total)
    stat_f[zl, 1:2] = weighted / total
    stat_f[zl, 2:8] = jnp.zeros((6, SPAN), jnp.float32)
    for z in z_peers:
        remote(stat_f.at[zl], stat_f.at[zl], f_send.at[0], f_recv.at[zl], at(zl=z)).start()

    def second_pass(zs):
        gain = jnp.exp(stat[zs, 0:1] - stat_f[zs, 0:1])
        p = pbuf[zs] * gain
        pb[zs] = p.astype(jnp.bfloat16)
        dsb[zs] = (p * (dbuf[zs] - stat_f[zs, 1:2])).astype(jnp.bfloat16)

    def each(k, _):
        zs = lax.rem(zl + k, NZ)

        @pl.when(k > 0)
        def _():
            remote(stat_f.at[zs], stat_f.at[zs], f_send.at[0], f_recv.at[zs], sibling).wait_recv()

        second_pass(zs)
        return 0

    lax.fori_loop(0, NZ, each, 0)

    def gradient(half, piece):
        first = pl.multiple_of(half * KEYS, KEYS)
        lo = piece * 256
        value = jnp.zeros((KEYS, 256), jnp.float32)
        key = jnp.zeros((KEYS, 256), jnp.float32)
        turn = jnp.zeros((KEYS, 128), jnp.float32)
        for k in range(NZ):
            chunk = rows.at[k * NY : (k + 1) * NY]
            ds_k = dsb[k, pl.ds(first, KEYS)]
            key = key + dot(ds_k, chunk[:, :, lo : lo + 256].reshape(SPAN, 256))
            value = value + dot(
                pb[k, pl.ds(first, KEYS)],
                chunk[:, :, VAL + lo : VAL + lo + 256].reshape(SPAN, 256),
            )
            if piece == 1:
                turn = turn + dot(ds_k, chunk[:, :, 2 * VAL : BLOCK].reshape(SPAN, 128))
        both = (key * score_scale + value).reshape(NX, 64, 256)
        tiles = [both[:, :, 0:128], both[:, :, 128:256]]
        if piece == 1:
            turn = (turn * score_scale).reshape(NX, 2, 32, 128)
            lane = lax.broadcasted_iota(jnp.int32, (NX, 32, 128), 2)
            tiles.append(jnp.where(lane < 64, turn[:, 0], turn[:, 1]))
        return jnp.concatenate(tiles, axis=1)

    for piece, (lo, size) in enumerate(SPLIT):
        s1[:, lo : lo + size] = gradient(1 - c, piece).astype(jnp.bfloat16)
        part = pl.ds(lo, size)
        remote(
            s1.at[:, part], r1.at[:, part], r1_send.at[piece], r1_recv.at[piece], sibling
        ).start()
    for piece, (lo, size) in enumerate(SPLIT):
        own = gradient(c, piece)
        part = pl.ds(lo, size)
        remote(
            s1.at[:, part], r1.at[:, part], r1_send.at[piece], r1_recv.at[piece], sibling
        ).wait()
        s2[:, lo : lo + size] = (own + r1[:, lo : lo + size].astype(jnp.float32)).astype(
            jnp.bfloat16
        )
        for k in x_peers:
            remote(
                s2.at[k, part], r2.at[x, part], r2_send.at[piece], r2_recv.at[piece, x], at(x=k)
            ).start()
    for piece, (lo, size) in enumerate(SPLIT):
        part = pl.ds(lo, size)
        for k in x_peers:
            remote(
                s2.at[k, part], r2.at[k, part], r2_send.at[piece], r2_recv.at[piece, k], at(x=k)
            ).wait_recv()
        total = s2[x, lo : lo + size].astype(jnp.float32)
        for k in x_peers:
            total = total + r2[k, lo : lo + size].astype(jnp.float32)
        s3[lo : lo + size] = total.astype(jnp.bfloat16)
        remote(s3.at[part], r3.at[part], r3_send.at[piece], r3_recv.at[piece], across).start()
    for piece, (lo, size) in enumerate(SPLIT):
        part = pl.ds(lo, size)
        remote(s3.at[part], r3.at[part], r3_send.at[piece], r3_recv.at[piece], across).wait()
        total = s3[lo : lo + size].astype(jnp.float32) + r3[lo : lo + size].astype(jnp.float32)
        fin[x, lo : lo + size] = total.astype(jnp.bfloat16)
        for k in x_peers:
            remote(
                fin.at[x, part], fin.at[x, part], r4_send.at[piece], r4_recv.at[piece, x], at(x=k)
            ).start()
    for piece, (lo, size) in enumerate(SPLIT):
        part = pl.ds(lo, size)
        for k in x_peers:
            remote(
                fin.at[k, part], fin.at[k, part], r4_send.at[piece], r4_recv.at[piece, k], at(x=k)
            ).wait_recv()
    for k in range(NX):
        for tile in range(4):
            out_ref[k * 64 : (k + 1) * 64, tile * 128 : (tile + 1) * 128] = fin[
                k, tile * 64 : (tile + 1) * 64
            ]
        out_ref[k * 64 : k * 64 + 32, VAL:LAT] = fin[k, 256:288, 0:64]
        out_ref[k * 64 + 32 : (k + 1) * 64, VAL:LAT] = fin[k, 256:288, 64:128]

    most = rows.at[pl.ds(0, NZ * NY - 1)]
    remote(most, most, g_send.at[0], g_recv.at[0], sibling).wait_send()
    swap.wait_send()
    for buffer, sem in ((stat, z_send), (stat_y, y_send), (stat_f, f_send)):
        seven = buffer.at[pl.ds(0, 7)]
        remote(seven, seven, sem.at[0], z_recv.at[0], sibling).wait_send()
    for piece, (lo, size) in enumerate(SPLIT):
        three = s2.at[pl.ds(0, 3), pl.ds(lo, size)]
        remote(three, three, r2_send.at[piece], r2_recv.at[piece, 0], sibling).wait_send()
        remote(three, three, r4_send.at[piece], r4_recv.at[piece, 0], sibling).wait_send()


def latent_gradient(query_pos, valid_keys, queries, output_gradient, latents):
    bf16, f32 = jnp.bfloat16, jnp.float32
    vmem, smem = pl.BlockSpec(memory_space=pltpu.VMEM), pl.BlockSpec(memory_space=pltpu.SMEM)
    dma = pltpu.SemaphoreType.DMA
    return pl.pallas_call(
        kernel,
        out_shape=jax.ShapeDtypeStruct((KEYS, LAT), bf16),
        in_specs=[smem, smem, vmem, vmem, vmem],
        out_specs=vmem,
        scratch_shapes=[
            pltpu.VMEM((NZ * NY, HEADS, BLOCK), bf16),
            pltpu.VMEM((2, KEYS, 640), bf16),
            pltpu.VMEM((2 * KEYS, 128), bf16),
            pltpu.VMEM((2 * KEYS, 128), f32),
            pltpu.VMEM((NZ, 2 * KEYS, SPAN), f32),
            pltpu.VMEM((NZ, 2 * KEYS, SPAN), f32),
            pltpu.VMEM((NZ, 2 * KEYS, SPAN), bf16),
            pltpu.VMEM((NZ, 2 * KEYS, SPAN), bf16),
            pltpu.VMEM((NZ, 8, SPAN), f32),
            pltpu.VMEM((NZ, 8, SPAN), f32),
            pltpu.VMEM((NY, 8, SPAN), f32),
            pltpu.VMEM((NZ, 8, SPAN), f32),
            pltpu.VMEM((NX, PART, 128), bf16),
            pltpu.VMEM((NX, PART, 128), bf16),
            pltpu.VMEM((NX, PART, 128), bf16),
            pltpu.VMEM((NX, PART, 128), bf16),
            pltpu.VMEM((PART, 128), bf16),
            pltpu.VMEM((PART, 128), bf16),
            pltpu.VMEM((NX, PART, 128), bf16),
            dma((NZ * NY,)), dma((1,)), dma((1,)), dma((1,)),
            dma((NZ,)), dma((1,)), dma((NY,)), dma((1,)), dma((NZ,)), dma((1,)),
            dma((2,)), dma((2,)), dma((2, NX)), dma((2,)),
            dma((2,)), dma((2,)), dma((2, NX)), dma((2,)),
        ],
        compiler_params=pltpu.CompilerParams(
            collective_id=0, has_side_effects=True, vmem_limit_bytes=40 * 2**20
        ),
        cost_estimate=pl.CostEstimate(
            flops=2_500_000_000, bytes_accessed=1_000_000, transcendentals=600_000
        ),
    )(query_pos, valid_keys, queries, output_gradient, latents)


def shards(queries, query_pos, latents, valid_keys, output_gradient, kv_down):
    latent_b = latent_gradient(query_pos, valid_keys, queries, output_gradient, latents)
    input_grad = lax.dot_general(
        latent_b, kv_down, (((1,), (1,)), ((), ())), preferred_element_type=jnp.float32
    ).astype(jnp.bfloat16)
    return (latent_b.astype(jnp.float32), input_grad)


def solution(mesh):
    torus = Mesh(mesh.devices.reshape(NX, 2, NZ, NY, 2), AXES)
    placed = (
        P(SEQ, HEAD, None),
        P(),
        P(SEQ, None),
        P(SEQ),
        P(SEQ, HEAD, None),
        P(HEAD, None),
    )
    return jax.shard_map(
        shards,
        mesh=torus,
        in_specs=placed,
        out_specs=(P(SEQ, None), P(SEQ, HEAD)),
        check_vma=False,
    )
```

time: 411 us -> 104 us (0.25)
  the two profiles are of different devices: /device:TPU:8 before, /device:TPU:64 now
where the time goes in v1:
time: 104 us
  Pallas kernels  99.3 us (95%)
  local copies, waits for them, and re-layouts  2.18 us (2%)
  between operations  1.44 us (1%)
  matrix products  1.31 us (1%)
    pallas_call x1, Pallas kernels, latent_gradient(): pl.pallas_call(kernel, out_shape=jax.ShapeDtypeStruct((KEYS, LAT), bf16),...  99.3 us
    unnamed x10, local copies, waits for them, and re-layouts  2.18 us

profile of v1, /device:TPU:64, one launch (start us, length us, event | category | flops | bytes accessed | tf_op | source)
XLA Modules:
  0.0 104.2 jit_solution(267229599467314089)
XLA Ops:
  0.6 0.0 copy-start
  1.4 0.0 copy-start.1
  1.4 0.0 copy-start.2
  1.4 0.0 copy-start.3
  1.4 1.2 %copy.8.lat_ref = bf16[256,576]{1,0:T(8,128)(2,1)S(1)} copy(bf16[256,576]{0,1:T(8,128)(2,1)} %param.8) | data formatting | bytes 589824 | tf_op args[2]
  2.6 0.0 copy-done.1
  2.6 0.0 copy-done.2
  2.6 0.0 copy-done.3
  2.6 99.3 %shard_map.77 = bf16[256,576]{1,0:T(8,128)(2,1)S(1)} custom-call(s32[128]{0:T(128)S(1)} %copy-done.3, s32[1]{0:T(128)S(6)} %copy.10.valid_ref, bf16[1,16,576]{2,1,0:T(8,128)(2,1)S(1)} %copy-done.1, bf16[1,16,512]{2,1,0:T(8,128)(2,1)S(1)} %copy-done.2, bf16[256,576]{1,0:T(8,128)(2,1)S(1)} %copy.8.lat_ref), custom_call_target="tpu_custom_call" | custom-call | flops 2500000000 | bytes 1000000 | tf_op jit(solution)/shard_map/pallas_call | solution.py:319
  101.9 0.0 copy-done
  101.9 1.3 %convolution_convert_fusion = bf16[256,896]{1,0:T(8,128)(2,1)} fusion(bf16[256,576]{1,0:T(8,128)(2,1)S(1)} %shard_map.77, bf16[896,576]{0,1:T(8,128)(2,1)S(1)} %copy-done), kind=kOutput, calls=%fused_computation | convolution fusion | flops 264470528 | bytes 1785856 | tf_op jit(solution)/shard_map/dot_general | solution.py:360
  103.2 1.0 copy.9
Async XLA Ops:
  0.6 101.3 %copy-start = (bf16[896,576]{0,1:T(8,128)(2,1)S(1)}, bf16[896,576]{0,1:T(8,128)(2,1)}, u32[]{:S(2)}) copy-start(bf16[896,576]{0,1:T(8,128)(2,1)} %param.11) | copy-start | bytes 3096580
  1.4 1.2 %copy-start.1 = (bf16[1,16,576]{2,1,0:T(8,128)(2,1)S(1)}, bf16[1,16,576]{2,1,0:T(8,128)(2,1)}, u32[]{:S(2)}) copy-start(bf16[1,16,576]{2,1,0:T(8,128)(2,1)} %q_ref.1) | copy-start | bytes 55300
  1.4 1.2 %copy-start.2 = (bf16[1,16,512]{2,1,0:T(8,128)(2,1)S(1)}, bf16[1,16,512]{2,1,0:T(8,128)(2,1)}, u32[]{:S(2)}) copy-start(bf16[1,16,512]{2,1,0:T(8,128)(2,1)} %g_ref.1) | copy-start | bytes 49156
  1.4 1.2 %copy-start.3 = (s32[128]{0:T(128)S(1)}, s32[128]{0:T(128)}, u32[]{:S(2)}) copy-start(s32[128]{0:T(128)} %qpos_ref.1) | copy-start | bytes 1540

commit v2 on v1

--- a/solution.py
+++ b/solution.py
@@ -15,11 +15,21 @@
 VAL = 512
 LAT = 576
 BLOCK = 1152
+GRAD = 640
+CUT = 1024
 SPAN = NY * HEADS
 PART = 288
 SPLIT = ((0, 128), (128, 160))
 MESH = pl.DeviceIdType.MESH
 
+ORDER = (
+    "y01", "z1", "y02", "p0", "z2", "y11", "z3", "y21", "r1", "y12", "z4", "y03",
+    "y31", "z5", "r2", "y22", "y13", "z6", "y41", "z7", "r3", "y04", "y32", "y51",
+    "c0", "y61", "y23", "r4", "y14", "y42", "y71", "c1", "y52", "y33", "y62", "r5",
+    "y24", "y43", "y72", "c2", "y53", "y34", "y63", "r6", "c3", "y73", "y44", "c4",
+    "y54", "c5", "y64", "c6", "y74", "r7", "c7",
+)
+
 score_scale = 192.0 ** (-0.5)
 
 
@@ -39,7 +49,7 @@
     qpos_ref, valid_ref, q_ref, g_ref, lat_ref, out_ref,
     rows, keys, krot, vis, pbuf, dbuf, pb, dsb, stat, stat_z, stat_y, stat_f,
     s1, r1, s2, r2, s3, r3, fin,
-    g_recv, g_send, k_recv, k_send, z_recv, z_send, y_recv, y_send, f_recv, f_send,
+    g_recv, g_send, h_recv, h_send, t_recv, t_send, k_recv, k_send, z_recv, z_send, y_recv, y_send, f_recv, f_send,
     r1_recv, r1_send, r2_recv, r2_send, r3_recv, r3_send, r4_recv, r4_send,
 ):
     x, zh, zl, y, c = (lax.axis_index(a) for a in AXES)
@@ -65,9 +75,9 @@
         pl.semaphore_signal(barrier, inc=1, device_id=peer, device_id_type=MESH)
 
     rows[mine, :, 0:VAL] = q_ref[0, :, 0:VAL]
-    rows[mine, :, VAL : 2 * VAL] = g_ref[0]
     rot = q_ref[0, :, VAL:LAT]
-    rows[mine, :, 2 * VAL : BLOCK] = jnp.concatenate([rot, rot], axis=1)
+    rows[mine, :, VAL:GRAD] = jnp.concatenate([rot, rot], axis=1)
+    rows[mine, :, GRAD:BLOCK] = g_ref[0]
     keys[c, :, 0:VAL] = lat_ref[:, 0:VAL]
     local = lax.broadcasted_iota(jnp.int32, (KEYS, 64), 0)
     flag = jnp.where(local < valid_ref[0], 1.0, 0.0).astype(jnp.bfloat16)
@@ -76,16 +86,50 @@
     pl.semaphore_wait(barrier, len(everyone))
 
     def send_rows(source, to):
-        remote(rows.at[source], rows.at[source], g_send.at[0], g_recv.at[source], to).start()
+        block = rows.at[source, :, pl.ds(0, CUT)]
+        remote(block, block, g_send.at[0], g_recv.at[source], to).start()
 
     def wait_rows(source):
-        remote(rows.at[source], rows.at[source], g_send.at[0], g_recv.at[source], sibling).wait_recv()
+        block = rows.at[source, :, pl.ds(0, CUT)]
+        remote(block, block, g_send.at[0], g_recv.at[source], sibling).wait_recv()
+
+    def rest_along_y(k):
+        block = rows.at[zl * NY + k, :, pl.ds(CUT, BLOCK - CUT)]
+        return block, h_send.at[0], h_recv.at[k]
+
+    def rest_along_z(zs, half):
+        block = rows.at[pl.ds(zs * NY + half * 4, 4), :, pl.ds(CUT, BLOCK - CUT)]
+        return block, t_recv.at[zs, half]
+
+    def rest_copies(zs, half):
+        block, recv = rest_along_z(zs, half)
+        up = remote(block, block, t_send.at[zs, half, 0], recv, at(zl=zl + 1))
+        down = remote(block, block, t_send.at[zs, half, 1], recv, at(zl=zl - 1))
+        return ((zs <= zl) & (zl + 1 < NZ), up), ((zs >= zl) & (zl - 1 >= 0), down)
+
+    def rest_send(zs, half):
+        for ok, copy in rest_copies(zs, half):
+            pl.when(ok)(copy.start)
+
+    def rest_relay(zs):
+        for half in range(2):
+            block, recv = rest_along_z(zs, half)
+            remote(block, block, t_send.at[0, 0, 0], recv, sibling).wait_recv()
+            rest_send(zs, half)
+
+    def rest_drain(zs):
+        for half in range(2):
+            for ok, copy in rest_copies(zs, half):
+                pl.when(ok)(copy.wait_send)
 
     send_rows(mine, at(y=y_up))
     send_rows(mine, at(y=y_down))
     for d in range(1, NZ):
         pl.when(zl + d < NZ)(lambda: send_rows(mine, at(zl=zl + d)))
         pl.when(zl - d >= 0)(lambda: send_rows(mine, at(zl=zl - d)))
+    block, send, recv = rest_along_y(y)
+    for peer in y_peers:
+        remote(block, block, send, recv, peer).start()
     swap = remote(keys.at[c], keys.at[c], k_send.at[0], k_recv.at[0], sibling)
     swap.start()
     swap.wait_recv()
@@ -99,7 +143,7 @@
         chunk = rows.at[pl.ds(zs * NY, NY)]
         values = keys[:, :, 0:VAL].reshape(2 * KEYS, VAL)
         s = dot_t(values, chunk[:, :, 0:VAL].reshape(SPAN, VAL))
-        s = s + dot_t(krot[...], chunk[:, :, 2 * VAL : BLOCK].reshape(SPAN, 128))
+        s = s + dot_t(krot[...], chunk[:, :, VAL:GRAD].reshape(SPAN, 128))
         lane = lax.broadcasted_iota(jnp.int32, (1, SPAN), 1)
         qpos = jnp.zeros((1, SPAN), jnp.int32)
         for k in range(NY):
@@ -109,7 +153,7 @@
         s = jnp.where(seen, s * score_scale, -1e30)
         top = jnp.maximum(jnp.max(s, axis=0, keepdims=True), -1e20)
         p = jnp.exp(s - top)
-        dp = dot_t(values, chunk[:, :, VAL : 2 * VAL].reshape(SPAN, VAL))
+        dp = dot_t(values, chunk[:, :, GRAD:BLOCK].reshape(SPAN, VAL))
         pbuf[zs] = p
         dbuf[zs] = dp
         stat[zs, 0:1] = top
@@ -123,23 +167,22 @@
                 stat.at[zs], stat_z.at[zl], z_send.at[0], z_recv.at[zl], at(zl=zs)
             ).start()
 
-    def slots(group, work):
+    def places(d, work):
         def body(k, _):
-            d = 2 * group + k // 2
-            zs = jnp.where(k % 2 == 0, zl + d, zl - d)
-            ok = (d >= 0) & (zs >= 0) & (zs < NZ) & ((d < NZ) & ((d > 0) | (k % 2 == 0)))
-            pl.when(ok)(lambda: work(zs))
+            zs = jnp.where(k == 0, zl + d, zl - d)
+            pl.when((zs >= 0) & (zs < NZ))(lambda: work(zs))
             return 0
 
-        lax.fori_loop(0, 4, body, 0)
+        if d == 0:
+            work(zl)
+        else:
+            lax.fori_loop(0, 2, body, 0)
 
     def inject(zs):
-        @pl.when(zs != zl)
-        def _():
-            source = zs * NY + y
-            wait_rows(source)
-            send_rows(source, at(y=y_up))
-            send_rows(source, at(y=y_down))
+        source = zs * NY + y
+        wait_rows(source)
+        send_rows(source, at(y=y_up))
+        send_rows(source, at(y=y_down))
 
     def pass_on(e):
         def work(zs):
@@ -162,14 +205,22 @@
 
         return work
 
-    def step(t, _):
-        slots(t, inject)
-        for e in range(1, 5):
-            pl.when((t - e >= 0) & (t - e <= 3))(lambda e=e: slots(t - e, pass_on(e)))
-        pl.when(t >= 4)(lambda: slots(t - 4, first_pass))
-        return 0
-
-    lax.fori_loop(0, 8, step, 0)
+    for event in ORDER:
+        kind, d = event[0], int(event[1])
+        if kind == "z":
+            places(d, inject)
+        elif kind == "y":
+            places(d, pass_on(int(event[2])))
+        elif kind == "r":
+            places(d, rest_relay)
+        elif kind == "c":
+            places(d, first_pass)
+        else:
+            for k in range(1, NY):
+                block, send, recv = rest_along_y(lax.rem(y + k, NY))
+                remote(block, block, send, recv, sibling).wait_recv()
+            for half in range(2):
+                rest_send(zl, half)
 
     def merged(parts):
         top = parts[0][0:1]
@@ -235,10 +286,10 @@
             key = key + dot(ds_k, chunk[:, :, lo : lo + 256].reshape(SPAN, 256))
             value = value + dot(
                 pb[k, pl.ds(first, KEYS)],
-                chunk[:, :, VAL + lo : VAL + lo + 256].reshape(SPAN, 256),
+                chunk[:, :, GRAD + lo : GRAD + lo + 256].reshape(SPAN, 256),
             )
             if piece == 1:
-                turn = turn + dot(ds_k, chunk[:, :, 2 * VAL : BLOCK].reshape(SPAN, 128))
+                turn = turn + dot(ds_k, chunk[:, :, VAL:GRAD].reshape(SPAN, 128))
         both = (key * score_scale + value).reshape(NX, 64, 256)
         tiles = [both[:, :, 0:128], both[:, :, 128:256]]
         if piece == 1:
@@ -300,7 +351,12 @@
         out_ref[k * 64 : k * 64 + 32, VAL:LAT] = fin[k, 256:288, 0:64]
         out_ref[k * 64 + 32 : (k + 1) * 64, VAL:LAT] = fin[k, 256:288, 64:128]
 
-    most = rows.at[pl.ds(0, NZ * NY - 1)]
+    for zs in range(NZ):
+        rest_drain(zs)
+    block, send, recv = rest_along_y(y)
+    seven = rows.at[pl.ds(0, 7), :, pl.ds(CUT, BLOCK - CUT)]
+    remote(seven, seven, send, recv, sibling).wait_send()
+    most = rows.at[pl.ds(0, NZ * NY - 1), :, pl.ds(0, CUT)]
     remote(most, most, g_send.at[0], g_recv.at[0], sibling).wait_send()
     swap.wait_send()
     for buffer, sem in ((stat, z_send), (stat_y, y_send), (stat_f, f_send)):
@@ -341,7 +397,8 @@
             pltpu.VMEM((PART, 128), bf16),
             pltpu.VMEM((PART, 128), bf16),
             pltpu.VMEM((NX, PART, 128), bf16),
-            dma((NZ * NY,)), dma((1,)), dma((1,)), dma((1,)),
+            dma((NZ * NY,)), dma((1,)), dma((NY,)), dma((1,)), dma((NZ, 2)), dma((NZ, 2, 2)),
+            dma((1,)), dma((1,)),
             dma((NZ,)), dma((1,)), dma((NY,)), dma((1,)), dma((NZ,)), dma((1,)),
             dma((2,)), dma((2,)), dma((2, NX)), dma((2,)),
             dma((2,)), dma((2,)), dma((2, NX)), dma((2,)),

time: 104 us -> 101 us (0.971)
  the two profiles are of different devices: /device:TPU:64 before, /device:TPU:120 now
where the time goes in v2:
time: 101 us
  Pallas kernels  95.7 us (95%)
  local copies, waits for them, and re-layouts  2.18 us (2%)
  between operations  1.44 us (1%)
  matrix products  1.31 us (1%)
    pallas_call x1, Pallas kernels, latent_gradient(): pl.pallas_call(kernel, out_shape=jax.ShapeDtypeStruct((KEYS, LAT), bf16),...  95.7 us
    unnamed x10, local copies, waits for them, and re-layouts  2.18 us

profile of v2, /device:TPU:120, one launch (start us, length us, event | category | flops | bytes accessed | tf_op | source)
XLA Modules:
  0.0 100.6 jit_solution(213037714631856060)
XLA Ops:
  0.6 0.0 copy-start
  1.4 0.0 copy-start.1
  1.4 0.0 copy-start.2
  1.4 0.0 copy-start.3
  1.4 1.2 %copy.8.lat_ref = bf16[256,576]{1,0:T(8,128)(2,1)S(1)} copy(bf16[256,576]{0,1:T(8,128)(2,1)} %param.8) | data formatting | bytes 589824 | tf_op args[2]
  2.6 0.0 copy-done.1
  2.6 0.0 copy-done.2
  2.6 0.0 copy-done.3
  2.6 95.7 %shard_map.77 = bf16[256,576]{1,0:T(8,128)(2,1)S(1)} custom-call(s32[128]{0:T(128)S(1)} %copy-done.3, s32[1]{0:T(128)S(6)} %copy.10.valid_ref, bf16[1,16,576]{2,1,0:T(8,128)(2,1)S(1)} %copy-done.1, bf16[1,16,512]{2,1,0:T(8,128)(2,1)S(1)} %copy-done.2, bf16[256,576]{1,0:T(8,128)(2,1)S(1)} %copy.8.lat_ref), custom_call_target="tpu_custom_call" | custom-call | flops 2500000000 | bytes 1000000 | tf_op jit(solution)/shard_map/pallas_call | solution.py:375
  98.3 0.0 copy-done
  98.3 1.3 %convolution_convert_fusion = bf16[256,896]{1,0:T(8,128)(2,1)} fusion(bf16[256,576]{1,0:T(8,128)(2,1)S(1)} %shard_map.77, bf16[896,576]{0,1:T(8,128)(2,1)S(1)} %copy-done), kind=kOutput, calls=%fused_computation | convolution fusion | flops 264470528 | bytes 1785856 | tf_op jit(solution)/shard_map/dot_general | solution.py:417
  99.6 1.0 copy.9
Async XLA Ops:
  0.6 97.7 %copy-start = (bf16[896,576]{0,1:T(8,128)(2,1)S(1)}, bf16[896,576]{0,1:T(8,128)(2,1)}, u32[]{:S(2)}) copy-start(bf16[896,576]{0,1:T(8,128)(2,1)} %param.11) | copy-start | bytes 3096580
  1.4 1.2 %copy-start.1 = (bf16[1,16,576]{2,1,0:T(8,128)(2,1)S(1)}, bf16[1,16,576]{2,1,0:T(8,128)(2,1)}, u32[]{:S(2)}) copy-start(bf16[1,16,576]{2,1,0:T(8,128)(2,1)} %q_ref.1) | copy-start | bytes 55300
  1.4 1.2 %copy-start.2 = (bf16[1,16,512]{2,1,0:T(8,128)(2,1)S(1)}, bf16[1,16,512]{2,1,0:T(8,128)(2,1)}, u32[]{:S(2)}) copy-start(bf16[1,16,512]{2,1,0:T(8,128)(2,1)} %g_ref.1) | copy-start | bytes 49156
  1.4 1.2 %copy-start.3 = (s32[128]{0:T(128)S(1)}, s32[128]{0:T(128)}, u32[]{:S(2)}) copy-start(s32[128]{0:T(128)} %qpos_ref.1) | copy-start | bytes 1540

commit v3 on v2

--- a/solution.py
+++ b/solution.py
@@ -23,11 +23,11 @@
 MESH = pl.DeviceIdType.MESH
 
 ORDER = (
-    "y01", "z1", "y02", "p0", "z2", "y11", "z3", "y21", "r1", "y12", "z4", "y03",
-    "y31", "z5", "r2", "y22", "y13", "z6", "y41", "z7", "r3", "y04", "y32", "y51",
-    "c0", "y61", "y23", "r4", "y14", "y42", "y71", "c1", "y52", "y33", "y62", "r5",
-    "y24", "y43", "y72", "c2", "y53", "y34", "y63", "r6", "c3", "y73", "y44", "c4",
-    "y54", "c5", "y64", "c6", "y74", "r7", "c7",
+    "y01", "z1", "p0", "y02", "z2", "y11", "z3", "y03", "r1", "z4", "y21", "z5",
+    "y12", "y31", "r2", "z6", "y41", "z7", "y51", "y22", "r3", "y32", "y61", "y42",
+    "y71", "y13", "y52", "r4", "y23", "y33", "y04", "y62", "y72", "y43", "c0", "r5",
+    "y14", "y53", "c1", "y63", "y24", "y34", "c3", "y73", "r6", "c2", "y44", "y54",
+    "c4", "c5", "y64", "c6", "y74", "r7", "c7",
 )
 
 score_scale = 192.0 ** (-0.5)
@@ -132,12 +132,14 @@
         remote(block, block, send, recv, peer).start()
     swap = remote(keys.at[c], keys.at[c], k_send.at[0], k_recv.at[0], sibling)
     swap.start()
-    swap.wait_recv()
-    for half in range(2):
-        tail = keys[half, :, VAL:640].astype(jnp.float32)
-        lane = lax.broadcasted_iota(jnp.int32, (KEYS, 128), 1)
-        krot[half * KEYS : (half + 1) * KEYS] = jnp.where(lane < 64, tail, 0.0).astype(jnp.bfloat16)
-        vis[half * KEYS : (half + 1) * KEYS] = jnp.broadcast_to(tail[:, 64:65], (KEYS, 128))
+
+    def take_keys():
+        swap.wait_recv()
+        for half in range(2):
+            tail = keys[half, :, VAL:640].astype(jnp.float32)
+            lane = lax.broadcasted_iota(jnp.int32, (KEYS, 128), 1)
+            krot[half * KEYS : (half + 1) * KEYS] = jnp.where(lane < 64, tail, 0.0).astype(jnp.bfloat16)
+            vis[half * KEYS : (half + 1) * KEYS] = jnp.broadcast_to(tail[:, 64:65], (KEYS, 128))
 
     def first_pass(zs):
         chunk = rows.at[pl.ds(zs * NY, NY)]
@@ -205,6 +207,7 @@
 
         return work
 
+    first = next(event for event in ORDER if event[0] == "c")
     for event in ORDER:
         kind, d = event[0], int(event[1])
         if kind == "z":
@@ -214,6 +217,8 @@
         elif kind == "r":
             places(d, rest_relay)
         elif kind == "c":
+            if event == first:
+                take_keys()
             places(d, first_pass)
         else:
             for k in range(1, NY):

time: 101 us -> 99.5 us (0.985)
  the two profiles are of different devices: /device:TPU:120 before, /device:TPU:64 now
where the time goes in v3:
time: 99.5 us; the launch traced here: 99.3 us
  Pallas kernels  94.4 us (95%)
  local copies, waits for them, and re-layouts  2.18 us (2%)
  between operations  1.44 us (1%)
  matrix products  1.31 us (1%)
    pallas_call x1, Pallas kernels, latent_gradient(): pl.pallas_call(kernel, out_shape=jax.ShapeDtypeStruct((KEYS, LAT), bf16),...  94.4 us
    unnamed x10, local copies, waits for them, and re-layouts  2.18 us

profile of v3, /device:TPU:64, one launch (start us, length us, event | category | flops | bytes accessed | tf_op | source)
XLA Modules:
  0.0 99.3 jit_solution(9173778156560752836)
XLA Ops:
  0.6 0.0 copy-start
  1.4 0.0 copy-start.1
  1.4 0.0 copy-start.2
  1.4 0.0 copy-start.3
  1.4 1.2 %copy.8.lat_ref = bf16[256,576]{1,0:T(8,128)(2,1)S(1)} copy(bf16[256,576]{0,1:T(8,128)(2,1)} %param.8) | data formatting | bytes 589824 | tf_op args[2]
  2.6 0.0 copy-done.1
  2.6 0.0 copy-done.2
  2.6 0.0 copy-done.3
  2.6 94.4 %shard_map.77 = bf16[256,576]{1,0:T(8,128)(2,1)S(1)} custom-call(s32[128]{0:T(128)S(1)} %copy-done.3, s32[1]{0:T(128)S(6)} %copy.10.valid_ref, bf16[1,16,576]{2,1,0:T(8,128)(2,1)S(1)} %copy-done.1, bf16[1,16,512]{2,1,0:T(8,128)(2,1)S(1)} %copy-done.2, bf16[256,576]{1,0:T(8,128)(2,1)S(1)} %copy.8.lat_ref), custom_call_target="tpu_custom_call" | custom-call | flops 2500000000 | bytes 1000000 | tf_op jit(solution)/shard_map/pallas_call | solution.py:380
  97.0 0.0 copy-done
  97.1 1.3 %convolution_convert_fusion = bf16[256,896]{1,0:T(8,128)(2,1)} fusion(bf16[256,576]{1,0:T(8,128)(2,1)S(1)} %shard_map.77, bf16[896,576]{0,1:T(8,128)(2,1)S(1)} %copy-done), kind=kOutput, calls=%fused_computation | convolution fusion | flops 264470528 | bytes 1785856 | tf_op jit(solution)/shard_map/dot_general | solution.py:422
  98.4 1.0 copy.9
Async XLA Ops:
  0.6 96.4 %copy-start = (bf16[896,576]{0,1:T(8,128)(2,1)S(1)}, bf16[896,576]{0,1:T(8,128)(2,1)}, u32[]{:S(2)}) copy-start(bf16[896,576]{0,1:T(8,128)(2,1)} %param.11) | copy-start | bytes 3096580
  1.4 1.2 %copy-start.1 = (bf16[1,16,576]{2,1,0:T(8,128)(2,1)S(1)}, bf16[1,16,576]{2,1,0:T(8,128)(2,1)}, u32[]{:S(2)}) copy-start(bf16[1,16,576]{2,1,0:T(8,128)(2,1)} %q_ref.1) | copy-start | bytes 55300
  1.4 1.2 %copy-start.2 = (bf16[1,16,512]{2,1,0:T(8,128)(2,1)S(1)}, bf16[1,16,512]{2,1,0:T(8,128)(2,1)}, u32[]{:S(2)}) copy-start(bf16[1,16,512]{2,1,0:T(8,128)(2,1)} %g_ref.1) | copy-start | bytes 49156
  1.4 1.2 %copy-start.3 = (s32[128]{0:T(128)S(1)}, s32[128]{0:T(128)}, u32[]{:S(2)}) copy-start(s32[128]{0:T(128)} %qpos_ref.1) | copy-start | bytes 1540
